TPU v7x, 32 devices: a whole 2x2x4 slice. The times are simulated.
32 devices in a mesh: groups: 2 (over y), field: 4 (over x, core), wave: 4 (over z).
Axes of the slice: x: 2, y: 2, z: 4, core: 2. Of those that a mesh axis runs over, the one named last changes fastest.
Arguments:
- mode_basis: bfloat16 [22, 512, 512], P(None, 'wave'), may hold values from -6 to 6
- coef_table: bfloat16 [4096, 22], replicated, may hold values from -1.5 to 1.5
- table_index: int32 [64], P(('groups', 'field')), parts along dimension 0, may hold values from 0 to 4095
- wave_lengths: float32 [8], P('wave'), may hold values from 0.32 to 1.05
- sed_table: float32 [1024, 8], replicated, may hold values from 0.05 to 1
- template_ids: int32 [64, 8], P(('groups', 'field')), parts along dimension 0, may hold values from 0 to 1023
Outputs:
- mixed: bfloat16 [64, 8, 256, 256], P(('groups', 'field'), None, 'wave'), parts along dimension 0
There are 2 independent parts, one for each index of `groups`. A program takes and returns all parts, laid end to end along the dimension named above; an argument that names none is the same for every part. Nothing has to cross between parts.
All inputs are finite; a program needn't handle non-finite values.
Results may differ from a plain program's by a relative error of at most 0.0065.
Values may be sent and summed in bfloat16 or wider, within the bound.
A program may use at most 128 MiB of HBM per device.

v0:
```python
import math

import jax
import jax.numpy as jnp
from jax import lax
from jax.sharding import PartitionSpec as P

PUP = 512
PIX = 256


TWO_PI = 2.0 * math.pi
SAMPLING = 0.25
EPSILON = 1e-06


def transform_table(wave_lengths, pixels, pupil_side):
    pixel_offset = jnp.arange(pixels, dtype=jnp.int32) - pixels // 2
    pupil_offset = 2 * jnp.arange(pupil_side, dtype=jnp.int32) - pupil_side + 1
    products = (pixel_offset[:, None] * pupil_offset[None, :]).astype(jnp.float32)
    factor = TWO_PI * SAMPLING / (2.0 * pupil_side) / wave_lengths
    angles = products[None, :, :] * factor[:, None, None]
    cosine = jnp.cos(angles)
    sine_part = jnp.sin(angles)
    upper_half = jnp.concatenate([cosine, sine_part], axis=2)
    lower_half = jnp.concatenate([-sine_part, cosine], axis=2)
    return jnp.concatenate([upper_half, lower_half], axis=1).astype(jnp.bfloat16)


def aperture_rows(row_start, row_count, pupil_side):
    row_pos = 2 * (row_start + jnp.arange(row_count, dtype=jnp.int32)) - pupil_side + 1
    col_pos = 2 * jnp.arange(pupil_side, dtype=jnp.int32) - pupil_side + 1
    radius_sq = row_pos[:, None] * row_pos[:, None] + col_pos[None, :] * col_pos[None, :]
    inner_edge = 61 * pupil_side // 100
    inside = (radius_sq <= pupil_side * pupil_side) & (radius_sq >= inner_edge * inner_edge)
    return inside.astype(jnp.float32)


def pupil_section(path_rows, wave_lengths, kernel_table, row_start):
    row_count = path_rows.shape[1]
    pupil_side = path_rows.shape[2]
    opening = aperture_rows(row_start, row_count, pupil_side)
    phase_map = path_rows[:, None, :, :] * (TWO_PI / wave_lengths)[None, :, None, None]
    field_real = opening * jnp.cos(phase_map)
    field_imag = opening * jnp.sin(phase_map)
    pupil_field = jnp.concatenate([field_real, field_imag], axis=3).astype(jnp.bfloat16)
    first_pass = jnp.einsum(
        "flxy,luy->flxu", pupil_field, kernel_table, preferred_element_type=jnp.float32
    )
    return first_pass.astype(jnp.bfloat16)


def finish_section(first_pass, kernel_table):
    pixels = first_pass.shape[3] // 2
    stacked = jnp.concatenate([first_pass[..., :pixels], first_pass[..., pixels:]], axis=2)
    image_field = jnp.einsum(
        "lux,flxv->fluv", kernel_table, stacked, preferred_element_type=jnp.float32
    )
    intensity = (
        image_field[:, :, :pixels] * image_field[:, :, :pixels]
        + image_field[:, :, pixels:] * image_field[:, :, pixels:]
    )
    mean_level = jnp.mean(intensity, axis=(2, 3), keepdims=True)
    return (intensity / (mean_level + EPSILON)).astype(jnp.bfloat16)


def local(mode_basis, coef_table, table_index, wave_lengths, sed_table, template_ids):
    kernel_table = transform_table(wave_lengths, PIX, PUP)
    table_rows = coef_table.shape[0]
    selector = (table_index[:, None] == jnp.arange(table_rows, dtype=jnp.int32)[None, :]).astype(
        jnp.bfloat16
    )
    coeffs = jnp.dot(selector, coef_table, preferred_element_type=jnp.float32).astype(jnp.bfloat16)
    mode_count = mode_basis.shape[0]
    positions = coeffs.shape[0]
    whole_basis = lax.all_gather(mode_basis, "wave", axis=1, tiled=True)
    path_diff = jnp.dot(
        coeffs, whole_basis.reshape(mode_count, -1), preferred_element_type=jnp.float32
    )
    path_diff = path_diff.reshape(positions, PUP, PUP)
    first_pass = pupil_section(path_diff, wave_lengths, kernel_table, 0)
    spectra = finish_section(first_pass, kernel_table)
    pixel_slabs = lax.all_to_all(spectra, "wave", split_axis=2, concat_axis=1, tiled=True)
    sed_rows = sed_table.shape[0]
    one_hot = (
        template_ids[:, :, None] == jnp.arange(sed_rows, dtype=jnp.int32)[None, None, :]
    ).astype(jnp.float32)
    raw_weights = jnp.einsum("fjn,nl->fjl", one_hot, sed_table, precision=lax.Precision.HIGHEST)
    weights = (raw_weights / jnp.sum(raw_weights, axis=2, keepdims=True)).astype(jnp.bfloat16)
    mixed = jnp.einsum("fjl,flrp->fjrp", weights, pixel_slabs, preferred_element_type=jnp.float32)
    return mixed.astype(jnp.bfloat16)


def solution(mesh):
    return jax.shard_map(
        local,
        mesh=mesh,
        in_specs=(
            P(None, "wave", None),
            P(),
            P(("groups", "field")),
            P("wave"),
            P(),
            P(("groups", "field"), None),
        ),
        out_specs=P(("groups", "field"), None, "wave", None),
        check_vma=False,
    )
```

profile of v0, /device:TPU:0, one launch (start us, length us, event | category | flops | bytes accessed | tf_op | source)
XLA Modules:
  0.0 431.0 jit_solution(3552195632405545953)
XLA Ops:
  6.5 0.0 copy-start
  6.5 0.0 all-gather.2.cloned.1.call-start
  6.5 0.7 all-gather.2.cloned.1.call-update
  7.3 0.7 broadcast_divide_fusion.1
  8.0 0.1 multiply_convert_fusion
  8.1 0.2 fusion.30
  8.3 4.1 fusion.22
  12.4 0.0 copy-start.3
  12.4 200.3 %all-gather.2.cloned.1.call-done = bf16[22,512,512]{2,1,0:T(8,128)(2,1)} async-done(((bf16[22,128,512]{2,1,0:T(8,128)(2,1)}), bf16[22,512,512]{2,1,0:T(8,128)(2,1)}) %all-gather.2.cloned.1.call-update) | async-done | bytes 11534352 | tf_op jit(solution)/shard_map/all_gather | solution.py:76
  212.7 10.0 %slice_bitcast_fusion = bf16[512,512,22]{1,0,2:T(8,128)(2,1)} fusion(bf16[22,512,512]{2,1,0:T(8,128)(2,1)} %all-gather.2.cloned.1.call-done), kind=kLoop, calls=%fused_computation.13 | loop fusion | bytes 23068672 | tf_op jit(solution)/shard_map/reshape.39
  222.7 0.0 copy-done
  222.7 0.0 copy-done.3
  222.7 24.2 %fusion.9 = f32[8,512,512]{2,0,1:T(8,128)} fusion(bf16[512,512,22]{1,0,2:T(8,128)(2,1)} %slice_bitcast_fusion, bf16[4096,22]{0,1:T(8,128)(2,1)S(1)} %copy-done, s32[8]{0:T(128)S(1)} %copy-done.3), kind=kOutput, calls=%fused_computation.11 | convolution fusion | flops 93749424 | bytes 20103200 | tf_op jit(solution)/shard_map/dot_general | solution.py:77
  247.0 8.2 %copy.20 = f32[8,512,512]{2,1,0:T(8,128)S(1)} copy(f32[8,512,512]{2,0,1:T(8,128)} %fusion.9) | data formatting | bytes 16777216 | tf_op jit(solution)/shard_map/dot_general | solution.py:77
  255.2 64.3 %fusion.2 = (bf16[8,2,512,512]{3,2,0,1:T(8,128)(2,1)}, bf16[8,2,512,512]{3,2,0,1:T(8,128)(2,1)}) fusion(f32[2]{0:T(128)S(1)} %get-tuple-element.13, f32[8,512,512]{2,1,0:T(8,128)S(1)} %copy.20, f32[512,512]{1,0:T(8,128)S(1)} %fusion.30), kind=kLoop, calls=%fused_computation.4 | loop fusion | flops 20971520 | bytes 26214408 | tf_op jit(solution)/shard_map/convert
  319.5 14.6 %convert_bitcast_fusion = bf16[8,2,512,512]{3,2,0,1:T(8,128)(2,1)} fusion(bf16[8,2,512,512]{3,2,0,1:T(8,128)(2,1)} %get-tuple-element.6, bf16[8,2,512,512]{3,2,0,1:T(8,128)(2,1)} %get-tuple-element.5, bf16[2,256,512]{2,1,0:T(8,128)(2,1)S(1)} %get-tuple-element.11, bf16[2,256,512]{2,1,0:T(8,128)(2,1)S(1)} %get-tuple-element.10, ...), kind=kOutput, calls=%fused_computation.18 | convolution fusion | flops 8636071936 | bytes 26738688 | tf_op jit(solution)/shard_map/flxy,luy->flxu/dot_general | solution.py:47
  334.1 5.8 %fusion.41 = (bf16[8,2,512,256]{3,2,0,1:T(8,128)(2,1)}, bf16[8,2,512,256]{3,2,0,1:T(8,128)(2,1)}) fusion(bf16[8,2,512,512]{3,2,0,1:T(8,128)(2,1)} %convert_bitcast_fusion), kind=kLoop, calls=%fused_computation.58 | loop fusion | bytes 16777216 | tf_op jit(solution)/shard_map/slice | solution.py:55
  339.9 11.0 %fusion.18 = f32[8,2,512,256]{2,3,0,1:T(8,128)} fusion(bf16[8,2,512,256]{3,2,0,1:T(8,128)(2,1)} %get-tuple-element.8, bf16[8,2,512,256]{3,2,0,1:T(8,128)(2,1)} %get-tuple-element.7, bf16[2,256,512]{2,1,0:T(8,128)(2,1)S(1)} %get-tuple-element.11, bf16[2,256,512]{2,1,0:T(8,128)(2,1)S(1)} %get-tuple-element.10, bf16[2,256,512]{2,1,0:T(8,128)(2,1)S(1)} %get-tuple-element.9), kind=kOutput, calls=%fused_computation.23 | convolution fusion | flops 4320133120 | bytes 18350080 | tf_op jit(solution)/shard_map/lux,flxv->fluv/dot_general | solution.py:56
  351.0 0.0 copy-start.2
  351.0 4.3 fusion.31
  355.3 1.6 copy-done.2
  356.8 0.8 divide_convert_fusion
  357.6 0.0 copy-start.4
  357.6 0.0 copy-start.5
  357.6 3.1 copy.22
  360.7 3.6 all-to-all-start
  364.3 0.0 copy-done.4
  364.3 0.0 copy-done.5
  364.3 1.0 fusion.32
  365.4 47.6 %all-to-all-done = bf16[8,2,256,256]{3,0,1,2:T(8,128)(2,1)S(1)} async-done(((bf16[8,2,256,256]{3,0,1,2:T(8,128)(2,1)}), bf16[8,2,256,256]{3,0,1,2:T(8,128)(2,1)S(1)}, u32[]{:S(2)}, u32[]{:S(2)}) %all-to-all-start) | async-done | bytes 2097184 | tf_op jit(solution)/shard_map/all_to_all | solution.py:83
  413.0 2.9 copy.24
  415.9 0.0 copy-start.1
  415.9 2.8 all_to_all.16
  418.7 2.0 convolution_convert_fusion
  420.7 3.5 copy.26
  424.2 0.0 copy-done.1
  (4 shorter events, 0.0 us)
Async XLA Ops:
  6.5 216.2 %copy-start = (bf16[4096,22]{0,1:T(8,128)(2,1)S(1)}, bf16[4096,22]{0,1:T(8,128)(2,1)}, u32[]{:S(2)}) copy-start(bf16[4096,22]{0,1:T(8,128)(2,1)} %param.7) | copy-start | bytes 540676
  6.5 206.2 %all-gather.2.cloned.1.call-start = ((), (), s32[]{:S(2)}) async-start(), calls=%async_computation.1 | async-start | bytes 14417920 | tf_op jit(solution)/shard_map/all_gather | solution.py:76
  12.4 210.3 %copy-start.3 = (s32[8]{0:T(128)S(1)}, s32[8]{0:T(128)}, u32[]{:S(2)}) copy-start(s32[8]{0:T(128)} %param.8) | copy-start | bytes 100
  351.0 5.8 %copy-start.2 = (f32[8,2,512,256]{2,3,0,1:T(8,128)S(1)}, f32[8,2,512,256]{2,3,0,1:T(8,128)}, u32[]{:S(2)}) copy-start(f32[8,2,512,256]{2,3,0,1:T(8,128)} %fusion.18) | copy-start | bytes 25165828
  357.6 6.7 %copy-start.4 = (f32[1024,8]{0,1:T(8,128)S(1)}, f32[1024,8]{0,1:T(8,128)}, u32[]{:S(2)}) copy-start(f32[1024,8]{0,1:T(8,128)} %param.10) | copy-start | bytes 98308
  357.6 6.7 %copy-start.5 = (s32[8,8]{1,0:T(8,128)S(1)}, s32[8,8]{1,0:T(8,128)}, u32[]{:S(2)}) copy-start(s32[8,8]{1,0:T(8,128)} %param.11) | copy-start | bytes 772
  360.7 52.3 %all-to-all-start = ((bf16[8,2,256,256]{3,0,1,2:T(8,128)(2,1)}), bf16[8,2,256,256]{3,0,1,2:T(8,128)(2,1)S(1)}, u32[]{:S(2)}, u32[]{:S(2)}) async-start(bf16[8,2,256,256]{3,0,1,2:T(8,128)(2,1)} %copy.22), calls=%async_computation | async-start | bytes 4194304 | tf_op jit(solution)/shard_map/all_to_all | solution.py:83
  415.9 8.3 %copy-start.1 = (bf16[4096,22]{0,1:T(8,128)(2,1)S(1)}, bf16[4096,22]{0,1:T(8,128)(2,1)}, u32[]{:S(2)}) copy-start(bf16[4096,22]{0,1:T(8,128)(2,1)} %param.7) | copy-start | bytes 540676
Sparse Core Ops, SparseCore 0:
  8.9 203.7 all-gather.1
where the time goes:
time: 431 us
  waiting for transfers between devices  249 us (58%)
  other arithmetic  74.5 us (17%)
  matrix products  52.9 us (12%)
  local copies, waits for them, and re-layouts  37.8 us (9%)
  between operations  13.5 us (3%)
    all_gather x1, waiting for transfers between devices, local(): whole_basis = lax.all_gather(mode_basis, 'wave', axis=1, tiled=True)  200 us
    another operation x2, other arithmetic  68.4 us
    all_to_all x1, waiting for transfers between devices, local(): lax.all_to_all(spectra, 'wave', split_axis=2, concat_axis=1, tiled=True)  47.6 us
    dot_general x1, matrix products, local(): jnp.dot(coeffs, whole_basis.reshape(mode_count, -1), preferred_element_ty...  24.2 us
    dot_general x1, matrix products, pupil_section(): jnp.einsum('flxy,luy->flxu', pupil_field, kernel_table, preferred_element...  14.6 us
    dot_general x1, matrix products, finish_section(): jnp.einsum('lux,flxv->fluv', kernel_table, stacked, preferred_element_typ...  11 us
    another operation x1, local copies, waits for them, and re-layouts  9.99 us
  transfers between devices with their start and end apart: 2, of which 2 were waited for; matrix products, arithmetic and copies ran while one was open for 1% of the time, Pallas kernels for 0%

commit v1 on v0

v1 whole, which is shorter than its diff:
```python
import functools

import jax
import jax.numpy as jnp
from jax import lax
from jax.experimental import pallas as pl
from jax.experimental.pallas import tpu as pltpu
from jax.sharding import PartitionSpec as P

PUP = 512
PIX = 256
EPSILON = 1e-06
GROUP = 16
ROUNDER = 12582912.0


def turns_sincos(turns):
    nearest = (turns + ROUNDER) - ROUNDER
    r = turns - nearest
    s = r * r
    a = r * SINE(s)
    b = COSINE(s)
    return 1.0 - a * a, a * b


def SINE(s):
    return SIN[0] + s * (SIN[1] + s * (SIN[2] + s * SIN[3]))


def COSINE(s):
    return COS[0] + s * (COS[1] + s * (COS[2] + s * (COS[3] + s * COS[4])))


SIN = (4.442879676818848, -7.307816505432129, 3.5977742671966553, -0.7911993861198425)
COS = (1.4142135381698608, -6.978850841522217, 5.739460468292236, -1.883557915687561, 0.3106880187988281)


def transform_kernel(
    waves, fields, inv_ref, mix_ref, basis_ref, power_ref, total_ref, path, image, opening, table, efield
):
    slab = pl.program_id(0)
    slabs = pl.num_programs(0)
    rows = basis_ref.shape[3]
    modes = basis_ref.shape[0] * basis_ref.shape[2]
    upix = power_ref.shape[1] // fields
    first_row = slab * rows
    first_pix = lax.axis_index("wave") * upix

    x = 2 * (first_row + lax.broadcasted_iota(jnp.int32, (rows, PUP), 0)) - PUP + 1
    y = 2 * lax.broadcasted_iota(jnp.int32, (rows, PUP), 1) - PUP + 1
    radius = x * x + y * y
    inner = 61 * PUP // 100
    inside = (radius <= PUP * PUP) & (radius >= inner * inner)
    opening[...] = inside.astype(jnp.float32).astype(jnp.bfloat16)

    for r in range(0, rows, GROUP):
        block = basis_ref[:, 0, :, r : r + GROUP, :].reshape(modes * GROUP, PUP)
        diff = jnp.dot(mix_ref[...], block, preferred_element_type=jnp.float32)
        path[:, r : r + GROUP, :] = diff.reshape(fields, GROUP, PUP)

    def pass_wave(wave, first):
        inv = inv_ref[wave]
        scale = inv * (0.25 / (2.0 * PUP))
        lane = lax.broadcasted_iota(jnp.int32, (upix, 2 * rows), 1)
        real = lane < rows
        xs = 2 * (first_row + jnp.where(real, lane, lane - rows)) - PUP + 1
        us = first_pix + lax.broadcasted_iota(jnp.int32, (upix, 2 * rows), 0) - PIX // 2
        cosine, sine = turns_sincos((us * xs).astype(jnp.float32) * scale)
        kernel = jnp.concatenate(
            [jnp.where(real, cosine, sine), jnp.where(real, -sine, cosine)], axis=0
        ).astype(jnp.bfloat16)
        for f in range(fields):
            slot = f % 2
            for r in range(0, rows, GROUP):
                cosine, sine = turns_sincos(path[f, r : r + GROUP, :] * inv)
                hole = opening[r : r + GROUP, :]
                efield[slot, r : r + GROUP, :] = cosine.astype(jnp.bfloat16) * hole
                efield[slot, rows + r : rows + r + GROUP, :] = sine.astype(jnp.bfloat16) * hole
            part = jnp.dot(kernel, efield[slot], preferred_element_type=jnp.float32)
            here = pl.ds(f * upix, upix)
            if first:
                image[wave, here, :PUP] = part[:upix]
                image[wave, here, PUP:] = part[upix:]
            else:
                image[wave, here, :PUP] += part[:upix]
                image[wave, here, PUP:] += part[upix:]

    @pl.when(slab == 0)
    def _():
        lax.fori_loop(0, waves, lambda l, c: (pass_wave(l, True), c)[1], 0)

    @pl.when(slab > 0)
    def _():
        lax.fori_loop(0, waves, lambda l, c: (pass_wave(l, False), c)[1], 0)

    @pl.when(slab == slabs - 1)
    def _():
        def finish(wave, carry):
            scale = inv_ref[wave] * (0.25 / (2.0 * PUP))
            step = 64
            for r in range(0, PUP, step):
                ys = 2 * (r + lax.broadcasted_iota(jnp.int32, (step, PIX), 0)) - PUP + 1
                vs = lax.broadcasted_iota(jnp.int32, (step, PIX), 1) - PIX // 2
                cosine, sine = turns_sincos((ys * vs).astype(jnp.float32) * scale)
                cosine = cosine.astype(jnp.bfloat16)
                table[r : r + step, :PIX] = cosine
                table[r : r + step, PIX:] = (-sine).astype(jnp.bfloat16)
                table[PUP + r : PUP + r + step, :PIX] = sine.astype(jnp.bfloat16)
                table[PUP + r : PUP + r + step, PIX:] = cosine
            half = fields * upix // 2
            for h in range(2):
                field = jnp.dot(
                    image[wave, h * half : (h + 1) * half, :].astype(jnp.bfloat16),
                    table[...],
                    preferred_element_type=jnp.float32,
                )
                re, im = field[:, :PIX], field[:, PIX:]
                power = re * re + im * im
                power_ref[wave, h * half : (h + 1) * half, :] = power
                sums = jnp.sum(power.reshape(fields // 2, upix, PIX), axis=1)
                total_ref[wave, h * (fields // 2) : (h + 1) * (fields // 2), :] = sums
            return carry

        lax.fori_loop(0, waves, finish, 0)


def mix_kernel(fields, power_ref, level_ref, weight_ref, out_ref):
    f = pl.program_id(0)
    waves = power_ref.shape[0]
    templates = out_ref.shape[1]
    step = 16
    for r in range(0, power_ref.shape[1], step):
        sums = [None] * templates
        for l in range(waves):
            spectrum = (power_ref[l, r : r + step, :] * level_ref[l * fields + f]).astype(jnp.bfloat16)
            spectrum = spectrum.astype(jnp.float32)
            for j in range(templates):
                term = spectrum * weight_ref[(f * templates + j) * waves + l]
                sums[j] = term if l == 0 else sums[j] + term
        for j in range(templates):
            out_ref[0, j, r : r + step, :] = sums[j].astype(jnp.bfloat16)


def local(sizes, mode_basis, coef_table, table_index, wave_lengths, sed_table, template_ids):
    slabs, field_parts, group_parts = sizes
    count, rows, _ = mode_basis.shape
    fields = table_index.shape[0]
    upix = PIX // slabs
    plane = field_parts * group_parts
    own = -(-count // plane)
    inverse = 1.0 / lax.all_gather(wave_lengths, "wave", axis=0, tiled=True)
    waves = inverse.shape[0]

    place = lax.axis_index("groups") * field_parts + lax.axis_index("field")
    padded = jnp.pad(mode_basis, ((0, plane * own - count), (0, 0), (0, 0)))
    piece = lax.dynamic_slice_in_dim(padded, place * own, own, 0)
    column = lax.all_gather(piece, "wave", axis=0)
    basis = lax.all_gather(column, ("groups", "field"), axis=0)

    coeffs = jnp.pad(jnp.take(coef_table, table_index, axis=0, mode="clip"), ((0, 0), (0, plane * own - count)))
    same = jnp.eye(GROUP, dtype=jnp.bfloat16)
    mix = (coeffs[:, None, :, None] * same[None, :, None, :]).reshape(fields * GROUP, -1)

    power, total = pl.pallas_call(
        functools.partial(transform_kernel, waves, fields),
        grid=(slabs,),
        in_specs=[
            pl.BlockSpec(memory_space=pltpu.SMEM),
            pl.BlockSpec(memory_space=pltpu.VMEM),
            pl.BlockSpec((plane, 1, own, rows, PUP), lambda s: (0, s, 0, 0, 0)),
        ],
        out_specs=[
            pl.BlockSpec((waves, fields * upix, PIX), lambda s: (0, 0, 0)),
            pl.BlockSpec((waves, fields, PIX), lambda s: (0, 0, 0)),
        ],
        out_shape=[
            jax.ShapeDtypeStruct((waves, fields * upix, PIX), jnp.float32),
            jax.ShapeDtypeStruct((waves, fields, PIX), jnp.float32),
        ],
        scratch_shapes=[
            pltpu.VMEM((fields, rows, PUP), jnp.float32),
            pltpu.VMEM((waves, fields * upix, 2 * PUP), jnp.float32),
            pltpu.VMEM((rows, PUP), jnp.bfloat16),
            pltpu.VMEM((2 * PUP, 2 * PIX), jnp.bfloat16),
            pltpu.VMEM((2, 2 * rows, PUP), jnp.bfloat16),
        ],
        compiler_params=pltpu.CompilerParams(vmem_limit_bytes=56 * 2**20),
    )(inverse, mix, basis)

    mean = lax.psum(jnp.sum(total, axis=2), "wave") / (PIX * PIX)
    level = (1.0 / (mean + EPSILON)).reshape(-1)
    raw = jnp.take(sed_table, template_ids, axis=0, mode="clip")
    weights = (raw / jnp.sum(raw, axis=2, keepdims=True)).astype(jnp.bfloat16).astype(jnp.float32)
    templates = template_ids.shape[1]
    return pl.pallas_call(
        functools.partial(mix_kernel, fields),
        grid=(fields,),
        in_specs=[
            pl.BlockSpec((waves, upix, PIX), lambda f: (0, f, 0)),
            pl.BlockSpec(memory_space=pltpu.SMEM),
            pl.BlockSpec(memory_space=pltpu.SMEM),
        ],
        out_specs=pl.BlockSpec((1, templates, upix, PIX), lambda f: (f, 0, 0, 0)),
        out_shape=jax.ShapeDtypeStruct((fields, templates, upix, PIX), jnp.bfloat16),
    )(power, level, weights.reshape(-1))


def solution(mesh):
    sizes = (mesh.shape["wave"], mesh.shape["field"], mesh.shape["groups"])
    return jax.shard_map(
        functools.partial(local, sizes),
        mesh=mesh,
        in_specs=(
            P(None, "wave", None),
            P(),
            P(("groups", "field")),
            P("wave"),
            P(),
            P(("groups", "field"), None),
        ),
        out_specs=P(("groups", "field"), None, "wave", None),
        check_vma=False,
    )
```

time: 431 us -> 235 us (0.55)
  waiting for transfers between devices: 249 us -> 97.3 us
  Pallas kernels: 0 us -> 93.3 us
  other arithmetic: 74.5 us -> 1.79 us
  matrix products: 52.9 us -> 0 us
  local copies, waits for them, and re-layouts: 37.8 us -> 7.2 us
  blocking collectives: 0 us -> 21.3 us
    all_gather x1 -> x2, waiting for transfers between devices: 200 us -> 97.2 us  [the longest x1 57 us: local(): basis = lax.all_gather(column, ('groups', 'field'), axis=0)]
    pallas_call x0 -> x2, Pallas kernels: none -> 93.3 us  [the longest x1 85.9 us: local(): pl.pallas_call(functools.partial(transform_kernel, waves, fields), grid=(...]
    another operation x2 -> x0, other arithmetic: 68.4 us -> none
    dot_general x5 -> x0, matrix products: 52.9 us -> none  [the longest x1 24.2 us: local(): jnp.dot(coeffs, whole_basis.reshape(mode_count, -1), preferred_element_ty...]
    all_to_all x1 -> x0, waiting for transfers between devices: 47.6 us -> none  [local(): lax.all_to_all(spectra, 'wave', split_axis=2, concat_axis=1, tiled=True)]
    psum x0 -> x1, blocking collectives: none -> 11.7 us  [local(): mean = lax.psum(jnp.sum(total, axis=2), 'wave') / (PIX * PIX)]
    another operation x1 -> x0, local copies, waits for them, and re-layouts: 9.99 us -> none
    unnamed x0 -> x1, blocking collectives: none -> 9.61 us
  transfers between devices with their start and end apart: 2 -> 2, of which waited for: 2 -> 2; matrix products, arithmetic and copies ran while one was open for 1% -> 2% of each run, Pallas kernels for 0% -> 0%
where the time goes in v1:
time: 235 us
  waiting for transfers between devices  97.3 us (41%)
  Pallas kernels  93.3 us (40%)
  blocking collectives  21.3 us (9%)
  between operations  14.2 us (6%)
  local copies, waits for them, and re-layouts  7.2 us (3%)
    pallas_call x1, Pallas kernels, local(): pl.pallas_call(functools.partial(transform_kernel, waves, fields), grid=(...  85.9 us
    all_gather x1, waiting for transfers between devices, local(): basis = lax.all_gather(column, ('groups', 'field'), axis=0)  57 us
    all_gather x1, waiting for transfers between devices, local(): column = lax.all_gather(piece, 'wave', axis=0)  40.3 us
    psum x1, blocking collectives, local(): mean = lax.psum(jnp.sum(total, axis=2), 'wave') / (PIX * PIX)  11.7 us
    unnamed x1, blocking collectives  9.61 us
    pallas_call x1, Pallas kernels, local(): pl.pallas_call(functools.partial(mix_kernel, fields), grid=(fields,), in_...  7.34 us
  transfers between devices with their start and end apart: 2, of which 2 were waited for; matrix products, arithmetic and copies ran while one was open for 2% of the time, Pallas kernels for 0%

profile of v1, /device:TPU:0, one launch (start us, length us, event | category | flops | bytes accessed | tf_op | source)
XLA Modules:
  0.0 235.1 jit_solution(14169937383785563660)
XLA Ops:
  6.5 0.0 copy-start.5
  6.5 0.0 copy-start.4
  6.5 0.0 copy-start
  6.5 0.0 all-gather.5.cloned.1.call-start
  6.5 0.0 copy-start.3
  6.5 1.8 pad_dynamic-slice_fusion
  8.4 0.0 copy-start.1
  8.4 0.0 copy-start.2
  8.4 0.0 all-gather.5.cloned.1.call-update
  8.4 0.0 all-gather.7.cloned.1.call-start
  8.5 40.3 %all-gather.5.cloned.1.call-done = bf16[12,128,512]{2,1,0:T(8,128)(2,1)} async-done(((bf16[3,128,512]{2,1,0:T(8,128)(2,1)}), bf16[12,128,512]{2,1,0:T(8,128)(2,1)}) %all-gather.5.cloned.1.call-update) | async-done | bytes 1572880 | tf_op jit(solution)/shard_map/all_gather | solution.py:157
  48.8 0.0 all-gather.7.cloned.1.call-update
  48.8 0.0 copy-done.5
  48.8 0.6 dynamic-slice
  50.0 0.0 copy-done.4
  50.1 0.2 dynamic-update-slice
  50.3 9.6 %all-reduce.2 = f32[8]{0:T(128)S(1)} all-reduce(f32[8]{0:T(128)S(1)} %dynamic-update-slice), channel_id=1, replica_groups=mesh['groups'=2,'field'=4,'wave'=4] {'wave'}, use_global_device_ids=true, to_apply=%add.2 | all-reduce | flops 8 | bytes 64
  59.9 0.0 copy-done
  59.9 0.5 copy.11
  60.4 0.0 copy-done.3
  60.4 0.6 gather_fusion
  61.0 0.1 broadcast_multiply_fusion
  61.1 1.2 mul.26.mix_ref
  62.3 0.0 copy-done.1
  62.3 0.2 copy.12
  62.5 0.0 copy-done.2
  62.5 0.1 reshape.36
  62.6 0.6 gather_fusion.1
  63.2 0.1 reduce.1
  63.3 0.1 reshape.47
  63.4 0.1 fusion.1
  63.5 0.7 reshape.25.weight_ref
  64.2 0.5 broadcast_divide_fusion.inv_ref
  64.7 57.0 %all-gather.7.cloned.1.call-done = bf16[32,3,128,512]{3,2,1,0:T(8,128)(2,1)} async-done(((bf16[4,3,128,512]{3,2,1,0:T(8,128)(2,1)}), bf16[32,3,128,512]{3,2,1,0:T(8,128)(2,1)}) %all-gather.7.cloned.1.call-update) | async-done | bytes 12582928 | tf_op jit(solution)/shard_map/all_gather | solution.py:158
  121.7 85.9 %shard_map.64 = (f32[8,512,256]{2,1,0:T(8,128)}, f32[8,8,256]{2,1,0:T(8,128)}) custom-call(f32[8]{0:T(128)} %broadcast_divide_fusion.inv_ref, bf16[128,384]{1,0:T(8,128)(2,1)} %mul.26.mix_ref, bf16[8,4,3,128,512]{4,3,2,1,0:T(8,128)(2,1)} %bitcast.11), custom_call_target="tpu_custom_call" | custom-call | tf_op jit(solution)/shard_map/pallas_call | solution.py:164
  207.6 0.9 reduce_sum.18
  208.5 11.7 %psum.7 = f32[8,8]{1,0:T(8,128)S(1)} all-reduce(f32[8,8]{1,0:T(8,128)S(1)} %reduce_sum.18), channel_id=1, replica_groups=mesh['groups'=2,'field'=4,'wave'=4] {'wave'}, use_global_device_ids=true, to_apply=%region_1.2 | all-reduce | flops 64 | bytes 512 | tf_op jit(solution)/shard_map/psum | solution.py:190
  220.2 0.6 reshape.24.level_ref
  220.9 7.3 %shard_map.65 = bf16[8,8,64,256]{3,2,1,0:T(8,128)(2,1)} custom-call(f32[8,512,256]{2,1,0:T(8,128)} %get-tuple-element.7.power_ref, f32[64]{0:T(128)} %reshape.24.level_ref, f32[512]{0:T(512)} %reshape.25.weight_ref), custom_call_target="tpu_custom_call" | custom-call | tf_op jit(solution)/shard_map/pallas_call | solution.py:195
  (6 shorter events, 0.0 us)
Async XLA Ops:
  6.5 42.3 %copy-start.5 = (u32[32]{0:T(128)S(1)}, u32[32]{0:T(128)}, u32[]{:S(2)}) copy-start(u32[32]{0:T(128)} %constant.38) | copy-start | bytes 388
  6.5 43.5 %copy-start.4 = (f32[2]{0:T(128)S(1)}, f32[2]{0:T(128)}, u32[]{:S(2)}) copy-start(f32[2]{0:T(128)} %param.9) | copy-start | bytes 28
  6.5 53.4 %copy-start = (bf16[4096,22]{0,1:T(8,128)(2,1)S(1)}, bf16[4096,22]{0,1:T(8,128)(2,1)}, u32[]{:S(2)}) copy-start(bf16[4096,22]{0,1:T(8,128)(2,1)} %param.7) | copy-start | bytes 540676
  6.5 42.2 %all-gather.5.cloned.1.call-start = ((), (), s32[]{:S(2)}) async-start(), calls=%async_computation | async-start | bytes 1966080 | tf_op jit(solution)/shard_map/all_gather | solution.py:157
  6.5 53.9 %copy-start.3 = (s32[8]{0:T(128)S(1)}, s32[8]{0:T(128)}, u32[]{:S(2)}) copy-start(s32[8]{0:T(128)} %param.8) | copy-start | bytes 100
  8.4 53.9 %copy-start.1 = (f32[1024,8]{0,1:T(8,128)S(1)}, f32[1024,8]{0,1:T(8,128)}, u32[]{:S(2)}) copy-start(f32[1024,8]{0,1:T(8,128)} %param.10) | copy-start | bytes 98308
  8.4 54.1 %copy-start.2 = (s32[8,8]{1,0:T(8,128)S(1)}, s32[8,8]{1,0:T(8,128)}, u32[]{:S(2)}) copy-start(s32[8,8]{1,0:T(8,128)} %param.11) | copy-start | bytes 772
  8.4 113.2 %all-gather.7.cloned.1.call-start = ((), (), s32[]{:S(2)}) async-start(), calls=%async_computation.1 | async-start | bytes 14155776 | tf_op jit(solution)/shard_map/all_gather | solution.py:158
Sparse Core Ops, SparseCore 0:
  8.9 39.7 all-gather.4
  50.6 70.9 all-gather.6

commit v2 on v1

v2 whole, which is shorter than its diff:
```python
import functools

import jax
import jax.numpy as jnp
from jax import lax
from jax.experimental import pallas as pl
from jax.experimental.pallas import tpu as pltpu
from jax.sharding import PartitionSpec as P

PUP = 512
PIX = 256
EPSILON = 1e-06
GROUP = 16
ROUNDER = 12582912.0


def turns_sincos(turns):
    nearest = (turns + ROUNDER) - ROUNDER
    r = turns - nearest
    s = r * r
    a = r * SINE(s)
    b = COSINE(s)
    return 1.0 - a * a, a * b


def SINE(s):
    return SIN[0] + s * (SIN[1] + s * (SIN[2] + s * SIN[3]))


def COSINE(s):
    return COS[0] + s * (COS[1] + s * (COS[2] + s * (COS[3] + s * COS[4])))


SIN = (4.442879676818848, -7.307816505432129, 3.5977742671966553, -0.7911993861198425)
COS = (1.4142135381698608, -6.978850841522217, 5.739460468292236, -1.883557915687561, 0.3106880187988281)


def hop(order, slabs):
    odd = order % 2
    return odd * ((order + 1) // 2) + (1 - odd) * (slabs - order // 2)


def psf_kernel(
    sizes, waves, fields, mix_ref, weight_ref, length_ref, basis_ref, out_ref,
    whole, inverse, path, image, table, efield, power, total, arrived,
    local_sem, wl_send, wl_recv, send1, recv1, send2, recv2, send3, recv3, sum_send, sum_recv,
):
    slabs, field_parts, group_parts = sizes
    count, rows, _ = basis_ref.shape
    modes = whole.shape[1]
    upix = PIX // slabs
    own_waves = waves // slabs
    x_parts = field_parts // 2
    chips = x_parts * group_parts
    own = modes // (2 * chips)
    templates = out_ref.shape[1]

    me = lax.axis_index("wave")
    part = lax.axis_index("field")
    core = part % 2
    chip = lax.axis_index("groups") * x_parts + part // 2
    first_pix = me * upix

    def wave_peer(shift):
        return {"wave": (me + shift) % slabs}

    def chip_peer(shift):
        other = (chip + shift) % chips
        return {"groups": other // x_parts, "field": (other % x_parts) * 2 + core}

    sibling = {"field": part + 1 - 2 * core}

    def remote(src, dst, send, recv, device):
        return pltpu.make_async_remote_copy(
            src_ref=src, dst_ref=dst, send_sem=send, recv_sem=recv,
            device_id=device, device_id_type=pl.DeviceIdType.MESH,
        )

    def from_slab(order):
        return (me + 2 * slabs - hop(order, slabs)) % slabs

    def piece(slab, of_chip):
        return whole.at[slab, pl.ds((core * chips + of_chip) * own, own)]

    def first_copy(order):
        shift = hop(order, slabs)
        mine = piece(me, chip)
        return remote(mine, mine, send1.at[order - 1], recv1.at[order - 1], wave_peer(shift))

    def first_landed(order):
        ref = piece(from_slab(order), chip)
        return remote(ref, ref, send1.at[order - 1], recv1.at[order - 1], wave_peer(hop(order, slabs)))

    def plane_copy(order, shift):
        ref = piece(from_slab(order), chip)
        at = (order - 1, shift - 1)
        return remote(ref, ref, send2.at[at], recv2.at[at], chip_peer(shift))

    def plane_landed(order, shift):
        ref = piece(from_slab(order), (chip + chips - shift) % chips)
        at = (order - 1, shift - 1)
        return remote(ref, ref, send2.at[at], recv2.at[at], chip_peer(shift))

    def core_copy(order, which):
        ref = whole.at[from_slab(order), pl.ds(which * chips * own, chips * own)]
        return remote(ref, ref, send3.at[order - 1], recv3.at[order - 1], sibling)

    def length_copy(shift, sender):
        ref = inverse.at[pl.ds(sender * own_waves, own_waves)]
        return remote(ref, ref, wl_send.at[shift - 1], wl_recv.at[shift - 1], wave_peer(shift))

    barrier = pltpu.get_barrier_semaphore()
    peers = [wave_peer(d) for d in range(1, slabs)] + [chip_peer(e) for e in range(1, chips)] + [sibling]
    for peer in peers:
        pl.semaphore_signal(barrier, inc=1, device_id=peer, device_id_type=pl.DeviceIdType.MESH)
    bring = pltpu.make_async_copy(basis_ref, whole.at[me, pl.ds(0, count)], local_sem)
    bring.start()
    if modes > count:
        whole[me, count:, :, :] = jnp.zeros((modes - count, rows, PUP), jnp.bfloat16)
    inverse[pl.ds(me * own_waves, own_waves)] = 1.0 / length_ref[...]
    pl.semaphore_wait(barrier, len(peers))
    for d in range(1, slabs):
        length_copy(d, me).start()
    bring.wait()
    first_copy(1).start()

    def clear(f, carry):
        for l in range(waves):
            image[l, pl.ds(f * upix, upix), :] = jnp.zeros((upix, 2 * PUP), jnp.float32)
        return carry

    lax.fori_loop(0, fields, clear, 0)
    for d in range(1, slabs):
        length_copy(d, (me + slabs - d) % slabs).wait_recv()

    def step_body(step, carry):
        order = step // waves
        wave = step % waves
        slab = from_slab(order)
        first_row = slab * rows

        for o in range(1, slabs):

            @pl.when(step == (o * 7 * waves) // 16)
            def _():
                first_landed(o).wait_recv()
                if o + 1 < slabs:
                    first_copy(o).wait_send()
                    first_copy(o + 1).start()
                for e in range(1, chips):
                    plane_copy(o, e).start()

            @pl.when(step == (o * waves - waves // 2 if o > 1 else waves))
            def _():
                for e in range(1, chips):
                    plane_landed(o, e).wait_recv()
                core_copy(o, core).start()

            @pl.when(step == o * waves)
            def _():
                core_copy(o, 1 - core).wait_recv()

        @pl.when(wave == 0)
        def _():
            def paths(g, c):
                r = pl.multiple_of(g * GROUP, GROUP)
                block = whole[slab, :, pl.ds(r, GROUP), :].reshape(modes * GROUP, PUP)
                diff = jnp.dot(mix_ref[...], block, preferred_element_type=jnp.float32)
                path[:, pl.ds(r, GROUP), :] = diff.reshape(fields, GROUP, PUP)
                x = 2 * (first_row + r + lax.broadcasted_iota(jnp.int32, (GROUP, PUP), 0)) - PUP + 1
                y = 2 * lax.broadcasted_iota(jnp.int32, (GROUP, PUP), 1) - PUP + 1
                radius = x * x + y * y
                inner = 61 * PUP // 100
                inside = (radius <= PUP * PUP) & (radius >= inner * inner)
                efield[2, pl.ds(r, GROUP), :] = inside.astype(jnp.float32).astype(jnp.bfloat16)
                return c

            lax.fori_loop(0, rows // GROUP, paths, 0)

        inv = inverse[wave]
        lane = lax.broadcasted_iota(jnp.int32, (upix, 2 * rows), 1)
        real = lane < rows
        xs = 2 * (first_row + jnp.where(real, lane, lane - rows)) - PUP + 1
        us = first_pix + lax.broadcasted_iota(jnp.int32, (upix, 2 * rows), 0) - PIX // 2
        scale = inv[:1, : 2 * rows] * (0.25 / (2.0 * PUP))
        cosine, sine = turns_sincos((us * xs).astype(jnp.float32) * scale)
        kernel = jnp.concatenate(
            [jnp.where(real, cosine, sine), jnp.where(real, -sine, cosine)], axis=0
        ).astype(jnp.bfloat16)
        for f in range(fields):
            slot = f % 2
            for r in range(0, rows, GROUP):
                cosine, sine = turns_sincos(path[f, r : r + GROUP, :] * inv[:1])
                hole = efield[2, r : r + GROUP, :]
                efield[slot, r : r + GROUP, :] = cosine.astype(jnp.bfloat16) * hole
                efield[slot, rows + r : rows + r + GROUP, :] = sine.astype(jnp.bfloat16) * hole
            part_sum = jnp.dot(kernel, efield[slot], preferred_element_type=jnp.float32)
            here = pl.ds(f * upix, upix)
            image[wave, here, :PUP] += part_sum[:upix]
            image[wave, here, PUP:] += part_sum[upix:]
        return carry

    lax.fori_loop(0, slabs * waves, step_body, 0)

    def finish(wave, carry):
        scale = inverse[wave][:1, :PIX] * (0.25 / (2.0 * PUP))
        step = 64
        for r in range(0, PUP, step):
            ys = 2 * (r + lax.broadcasted_iota(jnp.int32, (step, PIX), 0)) - PUP + 1
            vs = lax.broadcasted_iota(jnp.int32, (step, PIX), 1) - PIX // 2
            cosine, sine = turns_sincos((ys * vs).astype(jnp.float32) * scale)
            cosine = cosine.astype(jnp.bfloat16)
            table[r : r + step, :PIX] = cosine
            table[r : r + step, PIX:] = (-sine).astype(jnp.bfloat16)
            table[PUP + r : PUP + r + step, :PIX] = sine.astype(jnp.bfloat16)
            table[PUP + r : PUP + r + step, PIX:] = cosine
        half = fields * upix // 2
        for h in range(2):
            field = jnp.dot(
                image[wave, h * half : (h + 1) * half, :].astype(jnp.bfloat16),
                table[...],
                preferred_element_type=jnp.float32,
            )
            re, im = field[:, :PIX], field[:, PIX:]
            bright = re * re + im * im
            power[wave, h * half : (h + 1) * half, :] = bright
            sums = jnp.sum(jnp.sum(bright.reshape(fields // 2, upix, PIX), axis=1), axis=1, keepdims=True)
            total[wave, h * (fields // 2) : (h + 1) * (fields // 2), :] = jnp.broadcast_to(
                sums, (fields // 2, PIX)
            )
        return carry

    lax.fori_loop(0, waves, finish, 0)

    def sum_copy(shift):
        return remote(
            total, arrived.at[shift - 1], sum_send.at[shift - 1], sum_recv.at[shift - 1], wave_peer(shift)
        )

    for d in range(1, slabs):
        sum_copy(d).start()
    for d in range(1, slabs):
        sum_copy(d).wait()
    everything = total[...]
    for d in range(1, slabs):
        everything = everything + arrived[d - 1]
    total[...] = 1.0 / (everything * (1.0 / (PIX * PIX)) + EPSILON)

    step = 16

    def mix_fields(f, carry):
        for r in range(0, upix, step):
            sums = [None] * templates
            for l in range(waves):
                level = total[l, pl.ds(f, 1), :]
                bright = power[l, pl.ds(pl.multiple_of(f * upix, step) + r, step), :]
                spectrum = (bright * level).astype(jnp.bfloat16).astype(jnp.float32)
                for j in range(templates):
                    term = spectrum * weight_ref[(f * templates + j) * waves + l]
                    sums[j] = term if l == 0 else sums[j] + term
            for j in range(templates):
                out_ref[f, j, r : r + step, :] = sums[j].astype(jnp.bfloat16)
        return carry

    lax.fori_loop(0, fields, mix_fields, 0)

    for d in range(1, slabs):
        length_copy(d, me).wait_send()
    first_copy(slabs - 1).wait_send()
    for o in range(1, slabs):
        for e in range(1, chips):
            plane_copy(o, e).wait_send()
        core_copy(o, core).wait_send()


def local(sizes, waves, mode_basis, coef_table, table_index, wave_lengths, sed_table, template_ids):
    slabs, field_parts, group_parts = sizes
    count, rows, _ = mode_basis.shape
    fields, templates = template_ids.shape
    upix = PIX // slabs
    plane = field_parts * group_parts
    chips = plane // 2
    own = -(-count // plane)
    modes = plane * own

    coeffs = jnp.take(coef_table, table_index, axis=0, mode="clip")
    coeffs = jnp.pad(coeffs, ((0, 0), (0, modes - count)))
    same = jnp.eye(GROUP, dtype=jnp.bfloat16)
    mix = (coeffs[:, None, :, None] * same[None, :, None, :]).reshape(fields * GROUP, -1)
    raw = jnp.take(sed_table, template_ids, axis=0, mode="clip")
    weights = (raw / jnp.sum(raw, axis=2, keepdims=True)).astype(jnp.bfloat16).astype(jnp.float32)
    lengths = jnp.broadcast_to(wave_lengths[:, None, None], (wave_lengths.shape[0], 8, PUP))
    hops = slabs - 1
    dma = pltpu.SemaphoreType.DMA

    return pl.pallas_call(
        functools.partial(psf_kernel, sizes, waves, fields),
        in_specs=[
            pl.BlockSpec(memory_space=pltpu.VMEM),
            pl.BlockSpec(memory_space=pltpu.SMEM),
            pl.BlockSpec(memory_space=pltpu.VMEM),
            pl.BlockSpec(memory_space=pl.ANY),
        ],
        out_specs=pl.BlockSpec(memory_space=pltpu.VMEM),
        out_shape=jax.ShapeDtypeStruct((fields, templates, upix, PIX), jnp.bfloat16),
        scratch_shapes=[
            pltpu.VMEM((slabs, modes, rows, PUP), jnp.bfloat16),
            pltpu.VMEM((waves, 8, PUP), jnp.float32),
            pltpu.VMEM((fields, rows, PUP), jnp.float32),
            pltpu.VMEM((waves, fields * upix, 2 * PUP), jnp.float32),
            pltpu.VMEM((2 * PUP, 2 * PIX), jnp.bfloat16),
            pltpu.VMEM((3, 2 * rows, PUP), jnp.bfloat16),
            pltpu.VMEM((waves, fields * upix, PIX), jnp.float32),
            pltpu.VMEM((waves, fields, PIX), jnp.float32),
            pltpu.VMEM((hops, waves, fields, PIX), jnp.float32),
            dma,
            dma((hops,)),
            dma((hops,)),
            dma((hops,)),
            dma((hops,)),
            dma((hops, chips - 1)),
            dma((hops, chips - 1)),
            dma((hops,)),
            dma((hops,)),
            dma((hops,)),
            dma((hops,)),
        ],
        compiler_params=pltpu.CompilerParams(
            vmem_limit_bytes=60 * 2**20, collective_id=0, has_side_effects=True
        ),
    )(mix, weights.reshape(-1), lengths, mode_basis)


def solution(mesh):
    sizes = (mesh.shape["wave"], mesh.shape["field"], mesh.shape["groups"])


    def whole_program(*args):
        return sharded(mesh, functools.partial(local, sizes, args[3].shape[0]))(*args)

    return whole_program


def sharded(mesh, body):
    return jax.shard_map(
        body,
        mesh=mesh,
        in_specs=(
            P(None, "wave", None),
            P(),
            P(("groups", "field")),
            P("wave"),
            P(),
            P(("groups", "field"), None),
        ),
        out_specs=P(("groups", "field"), None, "wave", None),
        check_vma=False,
    )
```

time: 235 us -> 140 us (0.60)
  waiting for transfers between devices: 97.3 us -> 0 us
  Pallas kernels: 93.3 us -> 127 us
  blocking collectives: 21.3 us -> 0 us
  between operations: 14.2 us -> 0.04 us
  local copies, waits for them, and re-layouts: 7.2 us -> 10.7 us
    all_gather x2 -> x0, waiting for transfers between devices: 97.2 us -> none  [the longest x1 57 us: local(): basis = lax.all_gather(column, ('groups', 'field'), axis=0)]
    pallas_call x2 -> x1, Pallas kernels: 93.3 us -> 127 us  [local(): pl.pallas_call(functools.partial(psf_kernel, sizes, waves, fields), in_sp...]
    psum x1 -> x0, blocking collectives: 11.7 us -> none  [local(): mean = lax.psum(jnp.sum(total, axis=2), 'wave') / (PIX * PIX)]
    unnamed x1 -> x0, blocking collectives: 9.61 us -> none
    unnamed x17 -> x3, local copies, waits for them, and re-layouts: 1.54 us -> 5.53 us
  transfers between devices with their start and end apart: 2 -> 0, of which waited for: 2 -> 0; matrix products, arithmetic and copies ran while one was open for 2% -> 0% of each run, Pallas kernels for 0% -> 0%
where the time goes in v2:
time: 140 us; the launch traced here: 138 us
  Pallas kernels  127 us (91%)
  local copies, waits for them, and re-layouts  10.7 us (8%)
    pallas_call x1, Pallas kernels, local(): pl.pallas_call(functools.partial(psf_kernel, sizes, waves, fields), in_sp...  127 us
    unnamed x3, local copies, waits for them, and re-layouts  5.53 us

profile of v2, /device:TPU:0, one launch (start us, length us, event | category | flops | bytes accessed | tf_op | source)
XLA Modules:
  0.0 138.3 jit_solution(1038920915883093717)
XLA Ops:
  0.0 0.8 reshape.33
  0.8 0.7 pad_clamp_fusion.1
  1.4 1.3 broadcast_in_dim.19.length_ref
  2.8 0.9 copy.10
  3.7 0.6 gather_fusion.1
  4.3 0.1 reduce.1
  4.4 0.1 reshape.42
  4.5 0.1 fusion.1
  4.6 0.7 reshape.22.weight_ref
  5.3 1.4 %copy.9 = bf16[4096,22]{1,0:T(8,128)(2,1)S(1)} copy(bf16[4096,22]{0,1:T(8,128)(2,1)} %param.7) | data formatting | bytes 360448 | tf_op args[1]
  6.7 0.6 gather_fusion
  7.3 0.1 broadcast_multiply_fusion
  7.4 1.2 mul.20.mix_ref
  8.6 126.6 %shard_map.64 = bf16[8,8,64,256]{3,2,1,0:T(8,128)(2,1)} custom-call(bf16[128,384]{1,0:T(8,128)(2,1)} %mul.20.mix_ref, f32[512]{0:T(512)} %reshape.22.weight_ref, f32[2,8,512]{2,1,0:T(8,128)} %broadcast_in_dim.19.length_ref, bf16[22,128,512]{2,1,0:T(8,128)(2,1)} %basis_ref.1), custom_call_target="tpu_custom_call" | custom-call | tf_op jit(solution)/shard_map/pallas_call | solution.py:296
  135.2 3.2 %copy.12 = bf16[8,8,64,256]{3,2,1,0:T(8,128)(2,1)} copy(bf16[8,8,64,256]{3,2,1,0:T(8,128)(2,1)} %shard_map.64) | data formatting | bytes 4194304
  (3 shorter events, 0.0 us)
